TPU v7x, 32 devices: a whole 2x2x4 slice. The times are simulated.
32 devices in a mesh: row: 4 (over y, x), col: 8 (over z, core).
Axes of the slice: x: 2, y: 2, z: 4, core: 2. Of those that a mesh axis runs over, the one named last changes fastest.
Arguments:
- tokens: bfloat16 [128, 256, 1024], P(('row', 'col')), may hold values from -7 to 7
- phi: bfloat16 [1024, 32], replicated, may hold values from -5 to 5
- w_in: bfloat16 [32, 1024, 2048], P(('row', 'col')), may hold values from -0.1875 to 0.1875
- w_out: bfloat16 [32, 2048, 1024], P(('row', 'col')), may hold values from -0.125 to 0.125
- cotangent: bfloat16 [128, 256, 1024], P(('row', 'col')), may hold values from -6 to 6
Outputs:
- mixed: bfloat16 [128, 256, 1024], P(('row', 'col'))
- grad_tokens: bfloat16 [128, 256, 1024], P(('row', 'col'))
- grad_phi: float32 [1024, 32], P(None, ('row', 'col'))
- grad_w_in: bfloat16 [32, 1024, 2048], P(('row', 'col'))
- grad_w_out: bfloat16 [32, 2048, 1024], P(('row', 'col'))
All inputs are finite; a program needn't handle non-finite values.
Results may differ from a plain program's by a relative error of at most 0.015.
Values may be sent and summed in bfloat16 or wider, within the bound.
A program may use at most 128 MiB of HBM per device.

v0:
```python
import math

import jax
import jax.numpy as jnp
from jax import lax
from jax.sharding import PartitionSpec as P


def gelu_parts(pre_act):
    const = math.sqrt(2.0 / math.pi)
    inner = const * (pre_act + 0.044715 * pre_act**3)
    tanh_val = jnp.tanh(inner)
    value = 0.5 * pre_act * (1.0 + tanh_val)
    slope = 0.5 * (1.0 + tanh_val) + 0.5 * pre_act * (1.0 - tanh_val * tanh_val) * const * (
        1.0 + 3.0 * 0.044715 * pre_act * pre_act
    )
    return (value, slope)


def send_slots(slots):
    return lax.all_to_all(slots, ("row", "col"), split_axis=1, concat_axis=1, tiled=True)


def return_results(slots):
    return lax.all_to_all(slots, ("row", "col"), split_axis=1, concat_axis=1, tiled=True)


def send_out_grads(slots):
    return lax.all_to_all(slots, ("row", "col"), split_axis=1, concat_axis=1, tiled=True)


def return_in_grads(slots):
    return lax.all_to_all(slots, ("row", "col"), split_axis=1, concat_axis=1, tiled=True)


def on_device(tokens, phi, w_in, w_out, cotangent):
    f32 = jnp.float32
    images, patches, feature_dim = tokens.shape
    logits = jnp.einsum("imd,ds->ims", tokens, phi, preferred_element_type=f32)
    dispatch = jax.nn.softmax(logits, axis=1)
    combine = jax.nn.softmax(logits, axis=2)
    dispatch_b = dispatch.astype(jnp.bfloat16)
    combine_b = combine.astype(jnp.bfloat16)
    slot_in = jnp.einsum("ims,imd->isd", dispatch_b, tokens, preferred_element_type=f32).astype(
        jnp.bfloat16
    )
    expert_in = send_slots(slot_in)
    expert_rows = expert_in.reshape(-1, feature_dim)
    weight_a = w_in[0]
    weight_b = w_out[0]
    pre_act = jnp.dot(expert_rows, weight_a, preferred_element_type=f32)
    value, slope = gelu_parts(pre_act)
    hidden = value.astype(jnp.bfloat16)
    expert_out = jnp.dot(hidden, weight_b, preferred_element_type=f32).astype(jnp.bfloat16)
    slot_out = return_results(expert_out.reshape(expert_in.shape))
    mixed = jnp.einsum("ims,isd->imd", combine_b, slot_out, preferred_element_type=f32).astype(
        jnp.bfloat16
    )
    d_slot_out = jnp.einsum(
        "ims,imd->isd", combine_b, cotangent, preferred_element_type=f32
    ).astype(jnp.bfloat16)
    grad_rows = send_out_grads(d_slot_out).reshape(-1, feature_dim)
    d_combine = jnp.einsum("imd,isd->ims", cotangent, slot_out, preferred_element_type=f32)
    d_logits_c = combine * (d_combine - jnp.sum(combine * d_combine, axis=2, keepdims=True))
    grad_b = jnp.einsum("rh,rd->hd", hidden, grad_rows, preferred_element_type=f32).astype(
        jnp.bfloat16
    )
    d_hidden = jnp.einsum("rd,hd->rh", grad_rows, weight_b, preferred_element_type=f32)
    d_pre = (d_hidden * slope).astype(jnp.bfloat16)
    grad_a = jnp.einsum("rd,rh->dh", expert_rows, d_pre, preferred_element_type=f32).astype(
        jnp.bfloat16
    )
    d_rows = jnp.einsum("rh,dh->rd", d_pre, weight_a, preferred_element_type=f32).astype(
        jnp.bfloat16
    )
    d_slot_in = return_in_grads(d_rows.reshape(expert_in.shape))
    d_dispatch = jnp.einsum("imd,isd->ims", tokens, d_slot_in, preferred_element_type=f32)
    d_logits = (
        d_logits_c + dispatch * (d_dispatch - jnp.sum(dispatch * d_dispatch, axis=1, keepdims=True))
    ).astype(jnp.bfloat16)
    grad_tokens = (
        jnp.einsum("ims,isd->imd", dispatch_b, d_slot_in, preferred_element_type=f32)
        + jnp.einsum("ims,ds->imd", d_logits, phi, preferred_element_type=f32)
    ).astype(jnp.bfloat16)
    phi_terms = jnp.einsum("imd,ims->ds", tokens, d_logits, preferred_element_type=f32)
    grad_phi = lax.psum_scatter(phi_terms, ("row", "col"), scatter_dimension=1, tiled=True)
    return (mixed, grad_tokens, grad_phi, grad_a[None], grad_b[None])


def solution(mesh):
    placed = (
        P(("row", "col"), None, None),
        P(),
        P(("row", "col"), None, None),
        P(("row", "col"), None, None),
        P(("row", "col"), None, None),
    )
    return jax.shard_map(
        on_device,
        mesh=mesh,
        in_specs=placed,
        out_specs=(
            P(("row", "col"), None, None),
            P(("row", "col"), None, None),
            P(None, ("row", "col")),
            P(("row", "col"), None, None),
            P(("row", "col"), None, None),
        ),
        check_vma=False,
    )
```

profile of v0, /device:TPU:0, one launch (start us, length us, event | category | flops | bytes accessed | tf_op | source)
XLA Modules:
  0.0 219.8 jit_solution(336582949832847394)
XLA Ops:
  7.2 1.6 copy-done
  8.8 1.6 fusion.52
  10.3 0.8 fusion.60
  11.6 0.9 copy.18
  12.5 7.3 %all-to-all-start = ((bf16[4,32,1024]{2,0,1:T(4,128)(2,1)}), bf16[4,32,1024]{2,0,1:T(4,128)(2,1)S(1)}, u32[]{:S(2)}, u32[]{:S(2)}) async-start(bf16[4,32,1024]{2,0,1:T(4,128)(2,1)} %copy.18), calls=%async_computation | async-start | bytes 524288 | tf_op jit(solution)/shard_map/all_to_all | solution.py:21
  19.8 0.7 fusion.61
  20.5 2.0 convolution_convert_fusion.1
  22.6 0.9 copy.22
  23.5 6.7 %all-to-all-done = bf16[4,32,1024]{2,0,1:T(4,128)(2,1)S(1)} async-done(((bf16[4,32,1024]{2,0,1:T(4,128)(2,1)}), bf16[4,32,1024]{2,0,1:T(4,128)(2,1)S(1)}, u32[]{:S(2)}, u32[]{:S(2)}) %all-to-all-start) | async-done | bytes 262176 | tf_op jit(solution)/shard_map/all_to_all | solution.py:21
  30.2 3.3 %all-to-all-start.2 = ((bf16[4,32,1024]{2,0,1:T(4,128)(2,1)}), bf16[4,32,1024]{2,0,1:T(4,128)(2,1)}, u32[]{:S(2)}, u32[]{:S(2)}) async-start(bf16[4,32,1024]{2,0,1:T(4,128)(2,1)} %copy.22), calls=%async_computation.2 | async-start | bytes 524288 | tf_op jit(solution)/shard_map/all_to_all | solution.py:29
  33.6 3.1 %fusion.10 = f32[128,2048]{1,0:T(8,128)S(1)} fusion(bf16[128,1024]{1,0:T(8,128)(2,1)S(1)} %bitcast.57, bf16[1,1024,2048]{2,1,0:T(8,128)(2,1)} %param.7), kind=kOutput, calls=%fused_computation.10 | convolution fusion | flops 536870912 | bytes 5505024 | tf_op jit(solution)/shard_map/dot_general | solution.py:51
  37.0 1.6 fusion.21
  38.6 5.3 %all-to-all-done.2 = bf16[4,32,1024]{2,0,1:T(4,128)(2,1)} async-done(((bf16[4,32,1024]{2,0,1:T(4,128)(2,1)}), bf16[4,32,1024]{2,0,1:T(4,128)(2,1)}, u32[]{:S(2)}, u32[]{:S(2)}) %all-to-all-start.2) | async-done | bytes 262176 | tf_op jit(solution)/shard_map/all_to_all | solution.py:29
  43.9 1.0 copy.23
  44.9 4.9 %fusion.15 = bf16[128,2048]{1,0:T(8,128)(2,1)} fusion(bf16[128,1024]{1,0:T(8,128)(2,1)S(1)} %bitcast.59, bf16[1,2048,1024]{2,1,0:T(8,128)(2,1)} %param.8, f32[128,2048]{1,0:T(8,128)S(1)} %fusion.10), kind=kOutput, calls=%fused_computation.16 | convolution fusion | flops 541851648 | bytes 6029312 | tf_op jit(solution)/shard_map/rd,hd->rh/dot_general | solution.py:68
  49.8 0.9 copy.20
  50.8 3.3 %all-to-all-start.1 = ((bf16[4,32,1024]{2,0,1:T(4,128)(2,1)}), bf16[4,32,1024]{2,0,1:T(4,128)(2,1)}, u32[]{:S(2)}, u32[]{:S(2)}) async-start(bf16[4,32,1024]{2,0,1:T(4,128)(2,1)} %copy.20), calls=%async_computation.1 | async-start | bytes 524288 | tf_op jit(solution)/shard_map/all_to_all | solution.py:25
  54.1 3.9 %fusion.18 = bf16[128,1024]{1,0:T(8,128)(2,1)S(1)} fusion(bf16[128,2048]{1,0:T(8,128)(2,1)} %fusion.15, bf16[1,1024,2048]{2,1,0:T(8,128)(2,1)} %param.7), kind=kOutput, calls=%fused_computation.22 | convolution fusion | flops 537001984 | bytes 4980736 | tf_op jit(solution)/shard_map/rh,dh->rd/dot_general | solution.py:73
  58.0 0.9 copy.24
  58.9 3.3 %convert_bitcast_fusion.1 = bf16[1,1024,2048]{2,1,0:T(8,128)(2,1)} fusion(bf16[128,1024]{1,0:T(8,128)(2,1)S(1)} %bitcast.58, bf16[128,2048]{1,0:T(8,128)(2,1)S(1)} %copy-done.1), kind=kOutput, calls=%fused_computation.13 | convolution fusion | flops 538968064 | bytes 4980736 | tf_op jit(solution)/shard_map/rd,rh->dh/dot_general | solution.py:70
  62.2 3.3 %convert_bitcast_fusion = bf16[1,2048,1024]{2,1,0:T(8,128)(2,1)} fusion(bf16[128,1024]{1,0:T(8,128)(2,1)S(1)} %bitcast.60, f32[128,2048]{1,0:T(8,128)S(1)} %fusion.10), kind=kOutput, calls=%fused_computation.12 | convolution fusion | flops 541327360 | bytes 5505024 | tf_op jit(solution)/shard_map/rh,rd->hd/dot_general | solution.py:65
  65.6 5.8 %all-to-all-start.3 = ((bf16[4,32,1024]{2,0,1:T(4,128)(2,1)}), bf16[4,32,1024]{2,0,1:T(4,128)(2,1)S(1)}, u32[]{:S(2)}, u32[]{:S(2)}) async-start(bf16[4,32,1024]{2,0,1:T(4,128)(2,1)} %copy.24), calls=%async_computation.3 | async-start | bytes 524288 | tf_op jit(solution)/shard_map/all_to_all | solution.py:33
  71.6 2.4 %convolution_bitcast_fusion.1 = f32[4,256,32]{1,2,0:T(8,128)S(1)} fusion(bf16[4,256,1024]{2,1,0:T(8,128)(2,1)} %param.9, bf16[4,32,1024]{2,0,1:T(4,128)(2,1)} %all-to-all-done.1), kind=kOutput, calls=%fused_computation.27 | convolution fusion | flops 67108864 | bytes 2490368 | tf_op jit(solution)/shard_map/imd,isd->ims/dot_general | solution.py:63
  74.0 1.0 fusion.32
  75.0 6.7 %all-to-all-done.3 = bf16[4,32,1024]{2,0,1:T(4,128)(2,1)S(1)} async-done(((bf16[4,32,1024]{2,0,1:T(4,128)(2,1)}), bf16[4,32,1024]{2,0,1:T(4,128)(2,1)S(1)}, u32[]{:S(2)}, u32[]{:S(2)}) %all-to-all-start.3) | async-done | bytes 262176 | tf_op jit(solution)/shard_map/all_to_all | solution.py:33
  81.7 0.7 convolution_bitcast_fusion
  82.5 1.2 convolution_bitcast_fusion.2
  83.7 2.8 %fusion.46 = f32[4,256,1024]{2,1,0:T(8,128)} fusion(bf16[4,32,1024]{2,0,1:T(4,128)(2,1)S(1)} %all-to-all-done.3, f32[4,32]{1,0:T(4,128)S(1)} %get-tuple-element.5, f32[4,256,32]{1,2,0:T(8,128)S(1)} %fusion.52), kind=kOutput, calls=%fused_computation.49 | convolution fusion | flops 67207552 | bytes 4588032 | tf_op jit(solution)/shard_map/ims,isd->imd/dot_general | solution.py:82
  86.5 4.5 %add_convert_fusion = bf16[4,256,1024]{2,1,0:T(8,128)(2,1)} fusion(f32[4,256,1024]{2,1,0:T(8,128)} %fusion.46, f32[4,256,32]{1,2,0:T(8,128)S(1)} %fusion.32, f32[4,256,32]{1,2,0:T(8,128)S(1)} %convolution_bitcast_fusion, bf16[1024,32]{0,1:T(8,128)(2,1)S(1)} %copy-done.5, f32[4,256,32]{1,2,0:T(8,128)S(1)} %copy-done.4, f32[4,32]{1,0:T(4,128)S(1)} %get-tuple-element.5), kind=kOutput, calls=%fused_computation.14 | convolution fusion | flops 69435776 | bytes 6750720 | tf_op jit(solution)/shard_map/ims,ds->imd/dot_general | solution.py:83
  91.0 3.0 %convolution_convert_fusion = bf16[4,256,1024]{2,1,0:T(8,128)(2,1)} fusion(bf16[4,32,1024]{2,0,1:T(4,128)(2,1)} %all-to-all-done.1, f32[4,256]{1,0:T(4,128)S(1)} %get-tuple-element.7, f32[4,256,32]{1,2,0:T(8,128)S(1)} %fusion.52), kind=kOutput, calls=%fused_computation.17 | convolution fusion | flops 68256800 | bytes 2494464 | tf_op jit(solution)/shard_map/ims,isd->imd/dot_general | solution.py:56
  94.1 117.5 %all-reduce.3.cloned.1.call-done = f32[1024,32]{0,1:T(8,128)} async-done(((f32[1024,32]{0,1:T(8,128)}), f32[1024,32]{0,1:T(8,128)}) %all-reduce.3.cloned.1.call-update) | async-done | bytes 131088
  211.6 1.4 constant_dynamic-slice_fusion
  (20 shorter events, 1.2 us)
Async XLA Ops:
  7.2 1.6 copy-start
  12.5 17.7 %all-to-all-start = ((bf16[4,32,1024]{2,0,1:T(4,128)(2,1)}), bf16[4,32,1024]{2,0,1:T(4,128)(2,1)S(1)}, u32[]{:S(2)}, u32[]{:S(2)}) async-start(bf16[4,32,1024]{2,0,1:T(4,128)(2,1)} %copy.18), calls=%async_computation | async-start | bytes 524288 | tf_op jit(solution)/shard_map/all_to_all | solution.py:21
  30.2 13.7 %all-to-all-start.2 = ((bf16[4,32,1024]{2,0,1:T(4,128)(2,1)}), bf16[4,32,1024]{2,0,1:T(4,128)(2,1)}, u32[]{:S(2)}, u32[]{:S(2)}) async-start(bf16[4,32,1024]{2,0,1:T(4,128)(2,1)} %copy.22), calls=%async_computation.2 | async-start | bytes 524288 | tf_op jit(solution)/shard_map/all_to_all | solution.py:29
  33.5 3.5 %copy-start.7 = (bf16[1,2048,1024]{2,1,0:T(8,128)(2,1)S(1)}, bf16[1,2048,1024]{2,1,0:T(8,128)(2,1)}, u32[]{:S(2)}) copy-start(bf16[1,2048,1024]{2,1,0:T(8,128)(2,1)} %param.8) | copy-start | bytes 12582916
  44.9 4.9 %copy-start.2 = (bf16[4,32,1024]{2,1,0:T(8,128)(2,1)}, bf16[4,32,1024]{2,1,0:T(8,128)(2,1)S(1)}, u32[]{:S(2)}) copy-start(bf16[4,32,1024]{2,1,0:T(8,128)(2,1)S(1)} %copy.23) | copy-start | bytes 786436
  44.9 4.9 %copy-start.6 = (bf16[128,1024]{1,0:T(8,128)(2,1)S(1)}, bf16[128,1024]{1,0:T(8,128)(2,1)}, u32[]{:S(2)}) copy-start(bf16[128,1024]{1,0:T(8,128)(2,1)} %fusion.21) | copy-start | bytes 786436
  50.8 14.8 %all-to-all-start.1 = ((bf16[4,32,1024]{2,0,1:T(4,128)(2,1)}), bf16[4,32,1024]{2,0,1:T(4,128)(2,1)}, u32[]{:S(2)}, u32[]{:S(2)}) async-start(bf16[4,32,1024]{2,0,1:T(4,128)(2,1)} %copy.20), calls=%async_computation.1 | async-start | bytes 524288 | tf_op jit(solution)/shard_map/all_to_all | solution.py:25
  54.1 4.9 %copy-start.1 = (bf16[128,2048]{1,0:T(8,128)(2,1)S(1)}, bf16[128,2048]{1,0:T(8,128)(2,1)}, u32[]{:S(2)}) copy-start(bf16[128,2048]{1,0:T(8,128)(2,1)} %fusion.15) | copy-start | bytes 1572868
  54.1 8.1 %copy-start.3 = (bf16[4,32,1024]{2,1,0:T(8,128)(2,1)S(1)}, bf16[4,32,1024]{2,1,0:T(8,128)(2,1)}, u32[]{:S(2)}) copy-start(bf16[4,32,1024]{2,1,0:T(8,128)(2,1)} %copy-done.2) | copy-start | bytes 786436
  65.6 16.9 %copy-start.4 = (f32[4,256,32]{1,2,0:T(8,128)S(1)}, f32[4,256,32]{1,2,0:T(8,128)}, u32[]{:S(2)}) copy-start(f32[4,256,32]{1,2,0:T(8,128)} %get-tuple-element.6) | copy-start | bytes 393220
  65.6 16.2 %all-to-all-start.3 = ((bf16[4,32,1024]{2,0,1:T(4,128)(2,1)}), bf16[4,32,1024]{2,0,1:T(4,128)(2,1)S(1)}, u32[]{:S(2)}, u32[]{:S(2)}) async-start(bf16[4,32,1024]{2,0,1:T(4,128)(2,1)} %copy.24), calls=%async_computation.3 | async-start | bytes 524288 | tf_op jit(solution)/shard_map/all_to_all | solution.py:33
  71.3 140.2 %all-reduce.3.cloned.1.call-start = ((), (), s32[]{:S(2)}) async-start(), calls=%async_computation.4 | async-start | bytes 262144
  75.0 11.5 %copy-start.5 = (bf16[1024,32]{0,1:T(8,128)(2,1)S(1)}, bf16[1024,32]{0,1:T(8,128)(2,1)}, u32[]{:S(2)}) copy-start(bf16[1024,32]{0,1:T(8,128)(2,1)} %param.6) | copy-start | bytes 196612
Sparse Core Ops, SparseCore 0:
  91.2 120.3 all-reduce.2
where the time goes:
time: 220 us
  waiting for transfers between devices  136 us (62%)
  matrix products  38.9 us (18%)
  starting transfers between devices  19.9 us (9%)
  between operations  14.2 us (6%)
  local copies, waits for them, and re-layouts  8.05 us (4%)
  other arithmetic  2.51 us (1%)
    unnamed x2, waiting for transfers between devices  118 us
    all_to_all x1, starting transfers between devices, send_slots(): lax.all_to_all(slots, ('row', 'col'), split_axis=1, concat_axis=1, tiled=...  7.3 us
    all_to_all x1, waiting for transfers between devices, send_slots(): lax.all_to_all(slots, ('row', 'col'), split_axis=1, concat_axis=1, tiled=...  6.71 us
    all_to_all x1, waiting for transfers between devices, return_in_grads(): lax.all_to_all(slots, ('row', 'col'), split_axis=1, concat_axis=1, tiled=...  6.69 us
    all_to_all x1, starting transfers between devices, return_in_grads(): lax.all_to_all(slots, ('row', 'col'), split_axis=1, concat_axis=1, tiled=...  5.76 us
    all_to_all x1, waiting for transfers between devices, send_out_grads(): lax.all_to_all(slots, ('row', 'col'), split_axis=1, concat_axis=1, tiled=...  5.3 us
    dot_general x1, matrix products, on_device(): jnp.einsum('rd,hd->rh', grad_rows, weight_b, preferred_element_type=f32)  4.91 us
    dot_general x1, matrix products, on_device(): jnp.einsum('ims,ds->imd', d_logits, phi, preferred_element_type=f32)  4.47 us
  transfers between devices with their start and end apart: 5, of which 4 were waited for; matrix products, arithmetic and copies ran while one was open for 12% of the time, Pallas kernels for 0%

commit v1 on v0

--- a/solution.py
+++ b/solution.py
@@ -82,8 +82,9 @@
         jnp.einsum("ims,isd->imd", dispatch_b, d_slot_in, preferred_element_type=f32)
         + jnp.einsum("ims,ds->imd", d_logits, phi, preferred_element_type=f32)
     ).astype(jnp.bfloat16)
-    phi_terms = jnp.einsum("imd,ims->ds", tokens, d_logits, preferred_element_type=f32)
-    grad_phi = lax.psum_scatter(phi_terms, ("row", "col"), scatter_dimension=1, tiled=True)
+    phi_terms = jnp.einsum("ims,imd->sd", d_logits, tokens, preferred_element_type=f32)
+    shares = lax.all_to_all(phi_terms, ("row", "col"), split_axis=0, concat_axis=0, tiled=True)
+    grad_phi = jnp.sum(shares, axis=0)[:, None]
     return (mixed, grad_tokens, grad_phi, grad_a[None], grad_b[None])
 
 

time: 220 us -> 96.7 us (0.44)
  waiting for transfers between devices: 136 us -> 23.9 us
  between operations: 14.2 us -> 0.78 us
  starting transfers between devices: 19.9 us -> 22.4 us
    unnamed x2 -> x0, waiting for transfers between devices: 118 us -> none
    all_to_all x0 -> x1, waiting for transfers between devices: none -> 5.14 us  [on_device(): lax.all_to_all(phi_terms, ('row', 'col'), split_axis=0, concat_axis=0, ti...]
    all_to_all x0 -> x1, starting transfers between devices: none -> 2.57 us  [on_device(): lax.all_to_all(phi_terms, ('row', 'col'), split_axis=0, concat_axis=0, ti...]
  transfers between devices with their start and end apart: 5 -> 5, of which waited for: 4 -> 4; matrix products, arithmetic and copies ran while one was open for 12% -> 27% of each run, Pallas kernels for 0% -> 0%
where the time goes in v1:
time: 96.7 us; the launch traced here: 96 us
  matrix products  38.3 us (40%)
  waiting for transfers between devices  23.9 us (25%)
  starting transfers between devices  22.4 us (23%)
  local copies, waits for them, and re-layouts  7.46 us (8%)
  other arithmetic  3.19 us (3%)
    all_to_all x1, starting transfers between devices, send_slots(): lax.all_to_all(slots, ('row', 'col'), split_axis=1, concat_axis=1, tiled=...  7.3 us
    all_to_all x1, waiting for transfers between devices, return_in_grads(): lax.all_to_all(slots, ('row', 'col'), split_axis=1, concat_axis=1, tiled=...  6.74 us
    all_to_all x1, waiting for transfers between devices, send_slots(): lax.all_to_all(slots, ('row', 'col'), split_axis=1, concat_axis=1, tiled=...  6.72 us
    all_to_all x1, starting transfers between devices, return_in_grads(): lax.all_to_all(slots, ('row', 'col'), split_axis=1, concat_axis=1, tiled=...  5.94 us
    all_to_all x1, waiting for transfers between devices, send_out_grads(): lax.all_to_all(slots, ('row', 'col'), split_axis=1, concat_axis=1, tiled=...  5.3 us
    all_to_all x1, waiting for transfers between devices, on_device(): lax.all_to_all(phi_terms, ('row', 'col'), split_axis=0, concat_axis=0, ti...  5.14 us
    dot_general x1, matrix products, on_device(): jnp.einsum('rd,hd->rh', grad_rows, weight_b, preferred_element_type=f32)  4.91 us
    dot_general x1, matrix products, on_device(): jnp.einsum('ims,ds->imd', d_logits, phi, preferred_element_type=f32)  4.47 us
  transfers between devices with their start and end apart: 5, of which 4 were waited for; matrix products, arithmetic and copies ran while one was open for 27% of the time, Pallas kernels for 0%

profile of v1, /device:TPU:0, one launch (start us, length us, event | category | flops | bytes accessed | tf_op | source)
XLA Modules:
  0.0 96.0 jit_solution(15714668310031138573)
XLA Ops:
  0.6 1.6 %copy-done = bf16[4,256,1024]{2,1,0:T(8,128)(2,1)S(1)} copy-done((bf16[4,256,1024]{2,1,0:T(8,128)(2,1)S(1)}, bf16[4,256,1024]{2,1,0:T(8,128)(2,1)}, u32[]{:S(2)}) %copy-start) | copy-done | bytes 2097176
  2.2 1.6 %fusion.52 = f32[4,256,32]{1,2,0:T(8,128)S(1)} fusion(bf16[4,256,1024]{2,1,0:T(8,128)(2,1)S(1)} %copy-done, bf16[1024,32]{0,1:T(8,128)(2,1)} %param.6), kind=kOutput, calls=%fused_computation.56 | convolution fusion | flops 67108864 | bytes 2293760 | tf_op jit(solution)/shard_map/imd,ds->ims/dot_general | solution.py:39
  3.8 0.8 fusion.60
  5.1 0.9 copy.19
  6.0 7.3 %all-to-all-start = ((bf16[4,32,1024]{2,0,1:T(4,128)(2,1)}), bf16[4,32,1024]{2,0,1:T(4,128)(2,1)S(1)}, u32[]{:S(2)}, u32[]{:S(2)}) async-start(bf16[4,32,1024]{2,0,1:T(4,128)(2,1)} %copy.19), calls=%async_computation | async-start | bytes 524288 | tf_op jit(solution)/shard_map/all_to_all | solution.py:21
  13.3 0.7 fusion.61
  14.0 2.0 %convolution_convert_fusion.1 = bf16[4,32,1024]{2,1,0:T(8,128)(2,1)S(1)} fusion(bf16[4,256,1024]{2,1,0:T(8,128)(2,1)} %param.9, f32[4,256]{1,0:T(4,128)S(1)} %get-tuple-element.7, f32[4,256,32]{1,2,0:T(8,128)S(1)} %fusion.52), kind=kOutput, calls=%fused_computation.20 | convolution fusion | flops 67339296 | bytes 2494464 | tf_op jit(solution)/shard_map/ims,imd->isd/dot_general | solution.py:59
  16.0 0.9 copy.23
  16.9 6.7 %all-to-all-done = bf16[4,32,1024]{2,0,1:T(4,128)(2,1)S(1)} async-done(((bf16[4,32,1024]{2,0,1:T(4,128)(2,1)}), bf16[4,32,1024]{2,0,1:T(4,128)(2,1)S(1)}, u32[]{:S(2)}, u32[]{:S(2)}) %all-to-all-start) | async-done | bytes 262176 | tf_op jit(solution)/shard_map/all_to_all | solution.py:21
  23.7 3.3 %all-to-all-start.2 = ((bf16[4,32,1024]{2,0,1:T(4,128)(2,1)}), bf16[4,32,1024]{2,0,1:T(4,128)(2,1)}, u32[]{:S(2)}, u32[]{:S(2)}) async-start(bf16[4,32,1024]{2,0,1:T(4,128)(2,1)} %copy.23), calls=%async_computation.2 | async-start | bytes 524288 | tf_op jit(solution)/shard_map/all_to_all | solution.py:29
  27.1 3.1 %fusion.10 = f32[128,2048]{1,0:T(8,128)S(1)} fusion(bf16[128,1024]{1,0:T(8,128)(2,1)S(1)} %bitcast.57, bf16[1,1024,2048]{2,1,0:T(8,128)(2,1)} %param.7), kind=kOutput, calls=%fused_computation.10 | convolution fusion | flops 536870912 | bytes 5505024 | tf_op jit(solution)/shard_map/dot_general | solution.py:51
  30.4 1.6 %fusion.21 = bf16[128,1024]{1,0:T(8,128)(2,1)} fusion(bf16[1,2048,1024]{2,1,0:T(8,128)(2,1)S(1)} %copy-done.7, f32[128,2048]{1,0:T(8,128)S(1)} %fusion.10), kind=kOutput, calls=%fused_computation.23 | convolution fusion | flops 539361280 | bytes 5505024 | tf_op jit(solution)/shard_map/dot_general | solution.py:54
  32.0 5.3 %all-to-all-done.2 = bf16[4,32,1024]{2,0,1:T(4,128)(2,1)} async-done(((bf16[4,32,1024]{2,0,1:T(4,128)(2,1)}), bf16[4,32,1024]{2,0,1:T(4,128)(2,1)}, u32[]{:S(2)}, u32[]{:S(2)}) %all-to-all-start.2) | async-done | bytes 262176 | tf_op jit(solution)/shard_map/all_to_all | solution.py:29
  37.3 1.0 %copy.24 = bf16[4,32,1024]{2,1,0:T(8,128)(2,1)S(1)} copy(bf16[4,32,1024]{2,0,1:T(4,128)(2,1)} %all-to-all-done.2) | data formatting | bytes 524288 | tf_op jit(solution)/shard_map/all_to_all | solution.py:29
  38.4 4.9 %fusion.15 = bf16[128,2048]{1,0:T(8,128)(2,1)} fusion(bf16[128,1024]{1,0:T(8,128)(2,1)S(1)} %bitcast.59, bf16[1,2048,1024]{2,1,0:T(8,128)(2,1)} %param.8, f32[128,2048]{1,0:T(8,128)S(1)} %fusion.10), kind=kOutput, calls=%fused_computation.16 | convolution fusion | flops 541851648 | bytes 6029312 | tf_op jit(solution)/shard_map/rd,hd->rh/dot_general | solution.py:68
  43.3 0.9 copy.21
  44.2 3.3 %all-to-all-start.1 = ((bf16[4,32,1024]{2,0,1:T(4,128)(2,1)}), bf16[4,32,1024]{2,0,1:T(4,128)(2,1)}, u32[]{:S(2)}, u32[]{:S(2)}) async-start(bf16[4,32,1024]{2,0,1:T(4,128)(2,1)} %copy.21), calls=%async_computation.1 | async-start | bytes 524288 | tf_op jit(solution)/shard_map/all_to_all | solution.py:25
  47.6 3.9 %fusion.18 = bf16[128,1024]{1,0:T(8,128)(2,1)S(1)} fusion(bf16[128,2048]{1,0:T(8,128)(2,1)} %fusion.15, bf16[1,1024,2048]{2,1,0:T(8,128)(2,1)} %param.7), kind=kOutput, calls=%fused_computation.22 | convolution fusion | flops 537001984 | bytes 4980736 | tf_op jit(solution)/shard_map/rh,dh->rd/dot_general | solution.py:73
  51.5 0.9 copy.25
  52.4 3.3 %convert_bitcast_fusion.1 = bf16[1,1024,2048]{2,1,0:T(8,128)(2,1)} fusion(bf16[128,1024]{1,0:T(8,128)(2,1)S(1)} %bitcast.58, bf16[128,2048]{1,0:T(8,128)(2,1)S(1)} %copy-done.1), kind=kOutput, calls=%fused_computation.13 | convolution fusion | flops 538968064 | bytes 4980736 | tf_op jit(solution)/shard_map/rd,rh->dh/dot_general | solution.py:70
  55.7 3.3 %convert_bitcast_fusion = bf16[1,2048,1024]{2,1,0:T(8,128)(2,1)} fusion(bf16[128,1024]{1,0:T(8,128)(2,1)S(1)} %bitcast.60, f32[128,2048]{1,0:T(8,128)S(1)} %fusion.10), kind=kOutput, calls=%fused_computation.12 | convolution fusion | flops 541327360 | bytes 5505024 | tf_op jit(solution)/shard_map/rh,rd->hd/dot_general | solution.py:65
  59.0 5.9 %all-to-all-start.3 = ((bf16[4,32,1024]{2,0,1:T(4,128)(2,1)}), bf16[4,32,1024]{2,0,1:T(4,128)(2,1)S(1)}, u32[]{:S(2)}, u32[]{:S(2)}) async-start(bf16[4,32,1024]{2,0,1:T(4,128)(2,1)} %copy.25), calls=%async_computation.3 | async-start | bytes 524288 | tf_op jit(solution)/shard_map/all_to_all | solution.py:33
  65.0 2.4 %convolution_bitcast_fusion.1 = f32[4,256,32]{1,2,0:T(8,128)S(1)} fusion(bf16[4,256,1024]{2,1,0:T(8,128)(2,1)} %param.9, bf16[4,32,1024]{2,0,1:T(4,128)(2,1)} %all-to-all-done.1), kind=kOutput, calls=%fused_computation.27 | convolution fusion | flops 67108864 | bytes 2490368 | tf_op jit(solution)/shard_map/imd,isd->ims/dot_general | solution.py:63
  67.4 1.0 %fusion.32 = f32[4,256,32]{1,2,0:T(8,128)S(1)} fusion(f32[4,256,32]{1,2,0:T(8,128)S(1)} %convolution_bitcast_fusion.1, f32[4,256,32]{1,2,0:T(8,128)} %get-tuple-element.8, f32[4,256]{1,0:T(4,128)S(1)} %get-tuple-element.7), kind=kOutput, calls=%fused_computation.35 | output fusion | flops 164895 | bytes 397312 | tf_op jit(solution)/shard_map/sub | solution.py:64
  68.4 6.7 %all-to-all-done.3 = bf16[4,32,1024]{2,0,1:T(4,128)(2,1)S(1)} async-done(((bf16[4,32,1024]{2,0,1:T(4,128)(2,1)}), bf16[4,32,1024]{2,0,1:T(4,128)(2,1)S(1)}, u32[]{:S(2)}, u32[]{:S(2)}) %all-to-all-start.3) | async-done | bytes 262176 | tf_op jit(solution)/shard_map/all_to_all | solution.py:33
  75.2 0.7 convolution_bitcast_fusion
  76.5 2.8 %fusion.46 = f32[4,256,1024]{2,1,0:T(8,128)} fusion(bf16[4,32,1024]{2,0,1:T(4,128)(2,1)S(1)} %all-to-all-done.3, f32[4,32]{1,0:T(4,128)S(1)} %get-tuple-element.5, f32[4,256,32]{1,2,0:T(8,128)S(1)} %fusion.52), kind=kOutput, calls=%fused_computation.49 | convolution fusion | flops 67207552 | bytes 4588032 | tf_op jit(solution)/shard_map/ims,isd->imd/dot_general | solution.py:82
  79.3 4.5 %add_convert_fusion = bf16[4,256,1024]{2,1,0:T(8,128)(2,1)} fusion(f32[4,256,1024]{2,1,0:T(8,128)} %fusion.46, f32[4,256,32]{1,2,0:T(8,128)S(1)} %fusion.32, f32[4,256,32]{1,2,0:T(8,128)S(1)} %convolution_bitcast_fusion, bf16[1024,32]{0,1:T(8,128)(2,1)S(1)} %copy-done.5, f32[4,256,32]{1,2,0:T(8,128)S(1)} %copy-done.4, f32[4,32]{1,0:T(4,128)S(1)} %get-tuple-element.5), kind=kOutput, calls=%fused_computation.14 | convolution fusion | flops 69435776 | bytes 6750720 | tf_op jit(solution)/shard_map/ims,ds->imd/dot_general | solution.py:83
  83.8 0.8 copy.29
  84.6 2.6 %all-to-all-start.4 = ((f32[32,1,1024]{2,1,0:T(1,128)}), f32[32,1,1024]{2,1,0:T(1,128)S(1)}, u32[]{:S(2)}, u32[]{:S(2)}) async-start(f32[32,1,1024]{2,1,0:T(1,128)} %copy.29), calls=%async_computation.4 | async-start | bytes 262144 | tf_op jit(solution)/shard_map/all_to_all | solution.py:86
  87.2 3.0 %convolution_convert_fusion = bf16[4,256,1024]{2,1,0:T(8,128)(2,1)} fusion(bf16[4,32,1024]{2,0,1:T(4,128)(2,1)} %all-to-all-done.1, f32[4,256]{1,0:T(4,128)S(1)} %get-tuple-element.7, f32[4,256,32]{1,2,0:T(8,128)S(1)} %fusion.52), kind=kOutput, calls=%fused_computation.17 | convolution fusion | flops 68256800 | bytes 2494464 | tf_op jit(solution)/shard_map/ims,isd->imd/dot_general | solution.py:56
  90.2 5.1 %all-to-all-done.4 = f32[32,1,1024]{2,1,0:T(1,128)S(1)} async-done(((f32[32,1,1024]{2,1,0:T(1,128)}), f32[32,1,1024]{2,1,0:T(1,128)S(1)}, u32[]{:S(2)}, u32[]{:S(2)}) %all-to-all-start.4) | async-done | bytes 131104 | tf_op jit(solution)/shard_map/all_to_all | solution.py:86
  (20 shorter events, 2.2 us)
Async XLA Ops:
  0.6 1.6 %copy-start = (bf16[4,256,1024]{2,1,0:T(8,128)(2,1)S(1)}, bf16[4,256,1024]{2,1,0:T(8,128)(2,1)}, u32[]{:S(2)}) copy-start(bf16[4,256,1024]{2,1,0:T(8,128)(2,1)} %param.5) | copy-start | bytes 6291460
  6.0 17.7 %all-to-all-start = ((bf16[4,32,1024]{2,0,1:T(4,128)(2,1)}), bf16[4,32,1024]{2,0,1:T(4,128)(2,1)S(1)}, u32[]{:S(2)}, u32[]{:S(2)}) async-start(bf16[4,32,1024]{2,0,1:T(4,128)(2,1)} %copy.19), calls=%async_computation | async-start | bytes 524288 | tf_op jit(solution)/shard_map/all_to_all | solution.py:21
  23.7 13.7 %all-to-all-start.2 = ((bf16[4,32,1024]{2,0,1:T(4,128)(2,1)}), bf16[4,32,1024]{2,0,1:T(4,128)(2,1)}, u32[]{:S(2)}, u32[]{:S(2)}) async-start(bf16[4,32,1024]{2,0,1:T(4,128)(2,1)} %copy.23), calls=%async_computation.2 | async-start | bytes 524288 | tf_op jit(solution)/shard_map/all_to_all | solution.py:29
  27.0 3.5 %copy-start.7 = (bf16[1,2048,1024]{2,1,0:T(8,128)(2,1)S(1)}, bf16[1,2048,1024]{2,1,0:T(8,128)(2,1)}, u32[]{:S(2)}) copy-start(bf16[1,2048,1024]{2,1,0:T(8,128)(2,1)} %param.8) | copy-start | bytes 12582916
  38.4 4.9 %copy-start.2 = (bf16[4,32,1024]{2,1,0:T(8,128)(2,1)}, bf16[4,32,1024]{2,1,0:T(8,128)(2,1)S(1)}, u32[]{:S(2)}) copy-start(bf16[4,32,1024]{2,1,0:T(8,128)(2,1)S(1)} %copy.24) | copy-start | bytes 786436
  38.4 4.9 %copy-start.6 = (bf16[128,1024]{1,0:T(8,128)(2,1)S(1)}, bf16[128,1024]{1,0:T(8,128)(2,1)}, u32[]{:S(2)}) copy-start(bf16[128,1024]{1,0:T(8,128)(2,1)} %fusion.21) | copy-start | bytes 786436
  44.2 14.8 %all-to-all-start.1 = ((bf16[4,32,1024]{2,0,1:T(4,128)(2,1)}), bf16[4,32,1024]{2,0,1:T(4,128)(2,1)}, u32[]{:S(2)}, u32[]{:S(2)}) async-start(bf16[4,32,1024]{2,0,1:T(4,128)(2,1)} %copy.21), calls=%async_computation.1 | async-start | bytes 524288 | tf_op jit(solution)/shard_map/all_to_all | solution.py:25
  47.5 4.9 %copy-start.1 = (bf16[128,2048]{1,0:T(8,128)(2,1)S(1)}, bf16[128,2048]{1,0:T(8,128)(2,1)}, u32[]{:S(2)}) copy-start(bf16[128,2048]{1,0:T(8,128)(2,1)} %fusion.15) | copy-start | bytes 1572868
  47.6 8.1 %copy-start.3 = (bf16[4,32,1024]{2,1,0:T(8,128)(2,1)S(1)}, bf16[4,32,1024]{2,1,0:T(8,128)(2,1)}, u32[]{:S(2)}) copy-start(bf16[4,32,1024]{2,1,0:T(8,128)(2,1)} %copy-done.2) | copy-start | bytes 786436
  59.0 16.9 %copy-start.4 = (f32[4,256,32]{1,2,0:T(8,128)S(1)}, f32[4,256,32]{1,2,0:T(8,128)}, u32[]{:S(2)}) copy-start(f32[4,256,32]{1,2,0:T(8,128)} %get-tuple-element.6) | copy-start | bytes 393220
  59.0 16.1 %all-to-all-start.3 = ((bf16[4,32,1024]{2,0,1:T(4,128)(2,1)}), bf16[4,32,1024]{2,0,1:T(4,128)(2,1)S(1)}, u32[]{:S(2)}, u32[]{:S(2)}) async-start(bf16[4,32,1024]{2,0,1:T(4,128)(2,1)} %copy.25), calls=%async_computation.3 | async-start | bytes 524288 | tf_op jit(solution)/shard_map/all_to_all | solution.py:33
  68.4 10.9 %copy-start.5 = (bf16[1024,32]{0,1:T(8,128)(2,1)S(1)}, bf16[1024,32]{0,1:T(8,128)(2,1)}, u32[]{:S(2)}) copy-start(bf16[1024,32]{0,1:T(8,128)(2,1)} %param.6) | copy-start | bytes 196612
  84.6 10.7 %all-to-all-start.4 = ((f32[32,1,1024]{2,1,0:T(1,128)}), f32[32,1,1024]{2,1,0:T(1,128)S(1)}, u32[]{:S(2)}, u32[]{:S(2)}) async-start(f32[32,1,1024]{2,1,0:T(1,128)} %copy.29), calls=%async_computation.4 | async-start | bytes 262144 | tf_op jit(solution)/shard_map/all_to_all | solution.py:86

commit v2 on v0

v2 whole, which is shorter than its diff:
```python
import functools
import math

import jax
import jax.numpy as jnp
from jax import lax
from jax.experimental import pallas as pl
from jax.experimental.pallas import tpu as pltpu
from jax.sharding import PartitionSpec as P

F32 = jnp.float32
BF16 = jnp.bfloat16
MESH = pl.DeviceIdType.MESH
SLAB = 16


def gelu_parts(pre_act):
    const = math.sqrt(2.0 / math.pi)
    inner = const * (pre_act + 0.044715 * pre_act**3)
    tanh_val = jnp.tanh(inner)
    value = 0.5 * pre_act * (1.0 + tanh_val)
    slope = 0.5 * (1.0 + tanh_val) + 0.5 * pre_act * (1.0 - tanh_val * tanh_val) * const * (
        1.0 + 3.0 * 0.044715 * pre_act * pre_act
    )
    return (value, slope)


def dot(a, b, dims):
    return lax.dot_general(a, b, (dims, ((), ())), preferred_element_type=F32)


NN = ((1,), (0,))
NT = ((1,), (1,))
TN = ((0,), (0,))


def permutation(minor, group):
    size = minor * group
    shift = minor.bit_length() - 1
    row = lax.broadcasted_iota(jnp.int32, (size, size), 0)
    column = lax.broadcasted_iota(jnp.int32, (size, size), 1)
    source = (row & (minor - 1)) * group + (row >> shift)
    return jnp.where(column == source, 1.0, 0.0).astype(BF16)


def permutation_back(minor, group):
    size = minor * group
    shift = minor.bit_length() - 1
    row = lax.broadcasted_iota(jnp.int32, (size, size), 0)
    column = lax.broadcasted_iota(jnp.int32, (size, size), 1)
    source = (column & (minor - 1)) * group + (column >> shift)
    return jnp.where(row == source, 1.0, 0.0).astype(BF16)


def exchange_kernel(
    n, cols, images,
    tok_hbm, phi_t, w_in_hbm, w_out_hbm, cot_hbm,
    x_ref, hid_ref, dpre_ref, g_ref, so_ref, dsi_ref, disp_b, comb_b, dl_b, gphi_ref,
    tok, cot, w_in, w_out, rows, slope, disp, comb, perm, perm_back,
    sends, recvs, send_phi, recv_phi,
    load_sem, send_sem, recv_sem,
):
    patches, dim = tok.shape[0] // images, tok.shape[1]
    hid = w_in.shape[1]
    group = min(32, n)
    chunks = SLAB // images
    lanes = dim // chunks
    me = lax.axis_index("row") * cols + lax.axis_index("col")

    loads = [
        pltpu.make_async_copy(src, dst, load_sem.at[k])
        for k, (src, dst) in enumerate(
            ((tok_hbm, tok), (cot_hbm, cot), (w_in_hbm, w_in), (w_out_hbm, w_out))
        )
    ]
    for load in loads:
        load.start()

    barrier = pltpu.get_barrier_semaphore()

    def greet(j, carry):
        d = lax.rem(me + j, n)
        pl.semaphore_signal(barrier, inc=1, device_id=(d // cols, lax.rem(d, cols)), device_id_type=MESH)
        return carry

    lax.fori_loop(1, n, greet, 0)

    def start(k, src, dst):
        def one(j, carry):
            d = lax.rem(me + j, n)
            pltpu.make_async_remote_copy(
                src_ref=src.at[d], dst_ref=dst.at[me],
                send_sem=send_sem.at[k], recv_sem=recv_sem.at[k],
                device_id=(d // cols, lax.rem(d, cols)), device_id_type=MESH,
            ).start()
            return carry

        lax.fori_loop(1, n, one, 0)
        dst[me] = src[me]

    def whole(k, src, dst):
        d = lax.rem(me + 1, n)
        return pltpu.make_async_remote_copy(
            src_ref=src.at[pl.ds(0, n - 1)], dst_ref=dst.at[pl.ds(0, n - 1)],
            send_sem=send_sem.at[k], recv_sem=recv_sem.at[k],
            device_id=(d // cols, lax.rem(d, cols)), device_id_type=MESH,
        )

    def pack(src, dst):
        for g in range(n // group):
            parts = [
                src[i * n + g * group : i * n + (g + 1) * group, q * lanes : (q + 1) * lanes]
                for q in range(chunks)
                for i in range(images)
            ]
            out = dot(perm[...], jnp.concatenate(parts, axis=0), NN).astype(BF16)
            dst[g * group : (g + 1) * group] = out.reshape(group, SLAB, lanes)

    def unpack(src, dst):
        for g in range(n // group):
            slab = src[g * group : (g + 1) * group].reshape(group * SLAB, lanes)
            out = dot(perm_back[...], slab, NN).astype(BF16)
            for q in range(chunks):
                for i in range(images):
                    at = (q * images + i) * group
                    dst[i * n + g * group : i * n + (g + 1) * group, q * lanes : (q + 1) * lanes] = out[
                        at : at + group
                    ]

    perm[...] = permutation(SLAB, group)
    perm_back[...] = permutation_back(SLAB, group)

    loads[0].wait()
    for i in range(images):
        mine = tok[i * patches : (i + 1) * patches]
        logits = dot(phi_t[...], mine, NT)
        e = jnp.exp(logits - jnp.max(logits, axis=1, keepdims=True))
        dispatch = e / jnp.sum(e, axis=1, keepdims=True)
        disp[i] = dispatch
        disp_b[i] = dispatch.astype(BF16)
        e = jnp.exp(logits - jnp.max(logits, axis=0, keepdims=True))
        combine = e / jnp.sum(e, axis=0, keepdims=True)
        comb[i] = combine
        comb_b[i] = combine.astype(BF16)
        rows[i * n : (i + 1) * n] = dot(dispatch.astype(BF16), mine, NN).astype(BF16)
    pack(rows, sends.at[0])
    pl.semaphore_wait(barrier, n - 1)
    start(0, sends.at[0], recvs.at[0])

    loads[1].wait()
    for i in range(images):
        mine = cot[i * patches : (i + 1) * patches]
        rows[i * n : (i + 1) * n] = dot(comb_b[i], mine, NN).astype(BF16)
    pack(rows, sends.at[1])
    start(1, sends.at[1], recvs.at[1])

    loads[2].wait()
    loads[3].wait()
    wide = min(512, hid)
    thin = min(256, dim)

    whole(0, sends.at[0], recvs.at[0]).wait_recv()
    unpack(recvs.at[0], x_ref)

    @pl.loop(0, hid // wide)
    def _(c):
        at = pl.ds(pl.multiple_of(c * wide, wide), wide)
        value, grad = gelu_parts(dot(x_ref[...], w_in[:, at], NN))
        hid_ref[:, at] = value.astype(BF16)
        slope[:, at] = grad

    @pl.loop(0, dim // thin)
    def _(c):
        at = pl.ds(pl.multiple_of(c * thin, thin), thin)
        rows[:, at] = dot(hid_ref[...], w_out[:, at], NN).astype(BF16)

    pack(rows, sends.at[2])
    start(2, sends.at[2], recvs.at[2])

    whole(1, sends.at[1], recvs.at[1]).wait_recv()
    unpack(recvs.at[1], g_ref)

    @pl.loop(0, hid // wide)
    def _(c):
        at = pl.ds(pl.multiple_of(c * wide, wide), wide)
        dpre_ref[:, at] = (dot(g_ref[...], w_out[at, :], NT) * slope[:, at]).astype(BF16)

    @pl.loop(0, dim // thin)
    def _(c):
        at = pl.ds(pl.multiple_of(c * thin, thin), thin)
        rows[:, at] = dot(dpre_ref[...], w_in[at, :], NT).astype(BF16)

    pack(rows, sends.at[3])
    start(3, sends.at[3], recvs.at[3])

    whole(2, sends.at[2], recvs.at[2]).wait_recv()
    unpack(recvs.at[2], so_ref)
    for i in range(images):
        d_combine = dot(so_ref[i * n : (i + 1) * n], cot[i * patches : (i + 1) * patches], NT)
        combine = comb[i]
        comb[i] = combine * (d_combine - jnp.sum(combine * d_combine, axis=0, keepdims=True))

    whole(3, sends.at[3], recvs.at[3]).wait_recv()
    unpack(recvs.at[3], dsi_ref)
    terms = jnp.zeros((n, dim), F32)
    for i in range(images):
        mine = tok[i * patches : (i + 1) * patches]
        d_dispatch = dot(dsi_ref[i * n : (i + 1) * n], mine, NT)
        dispatch = disp[i]
        d_logits = comb[i] + dispatch * (
            d_dispatch - jnp.sum(dispatch * d_dispatch, axis=1, keepdims=True)
        )
        d_logits = d_logits.astype(BF16)
        dl_b[i] = d_logits
        terms = terms + dot(d_logits, mine, NN)

    minor = dim // 128
    phi_perm = permutation(minor, group)
    for g in range(n // group):
        some = terms[g * group : (g + 1) * group]
        flat = jnp.concatenate([some[:, j * 128 : (j + 1) * 128] for j in range(minor)], axis=0)
        high = flat.astype(BF16)
        rest = flat - high.astype(F32)
        middle = rest.astype(BF16)
        low = (rest - middle.astype(F32)).astype(BF16)
        out = dot(phi_perm, jnp.concatenate([high, middle, low], axis=1), NN)
        out = (out[:, :128] + out[:, 128:256]) + out[:, 256:]
        send_phi[g * group : (g + 1) * group] = out.reshape(group, minor, 128)
    start(4, send_phi, recv_phi)
    whole(4, send_phi, recv_phi).wait_recv()
    gphi_ref[...] = jnp.sum(recv_phi[...], axis=0)

    for k in range(4):
        whole(k, sends.at[k], recvs.at[k]).wait_send()
    whole(4, send_phi, recv_phi).wait_send()


def outputs_kernel(
    x_ref, dpre_ref, hid_ref, g_ref, comb_b, so_ref, disp_b, dl_b, dsi_ref, phi_t,
    mixed_ref, gtok_ref, gin_ref, gout_ref,
):
    gin_ref[0] = dot(x_ref[...], dpre_ref[...], TN).astype(BF16)
    gout_ref[0] = dot(hid_ref[...], g_ref[...], TN).astype(BF16)
    mixed_ref[0] = dot(comb_b[0], so_ref[...], TN).astype(BF16)
    left = jnp.concatenate([disp_b[0], dl_b[0]], axis=0)
    right = jnp.concatenate([dsi_ref[...], phi_t[...]], axis=0)
    gtok_ref[0] = dot(left, right, TN).astype(BF16)


def on_device(n, cols, tokens, phi, w_in, w_out, cotangent):
    images, patches, dim = tokens.shape
    hid = w_in.shape[2]
    count = images * n
    group = min(32, n)
    lanes = dim * images // SLAB
    minor = dim // 128
    phi_t = phi.T
    any_ = pl.BlockSpec(memory_space=pl.ANY)
    vmem = pl.BlockSpec(memory_space=pltpu.VMEM)

    def shape(*s, t=BF16):
        return jax.ShapeDtypeStruct(s, t)

    x, hidden, d_pre, grads, so, dsi, disp_b, comb_b, dl_b, gphi = pl.pallas_call(
        functools.partial(exchange_kernel, n, cols, images),
        out_shape=(
            shape(count, dim), shape(count, hid), shape(count, hid), shape(count, dim),
            shape(count, dim), shape(count, dim),
            shape(images, n, patches), shape(images, n, patches), shape(images, n, patches),
            shape(minor, 128, t=F32),
        ),
        in_specs=[any_, vmem, any_, any_, any_],
        out_specs=(vmem,) * 10,
        scratch_shapes=[
            pltpu.VMEM((images * patches, dim), BF16),
            pltpu.VMEM((images * patches, dim), BF16),
            pltpu.VMEM((dim, hid), BF16),
            pltpu.VMEM((hid, dim), BF16),
            pltpu.VMEM((count, dim), BF16),
            pltpu.VMEM((count, hid), F32),
            pltpu.VMEM((images, n, patches), F32),
            pltpu.VMEM((images, n, patches), F32),
            pltpu.VMEM((SLAB * group, SLAB * group), BF16),
            pltpu.VMEM((SLAB * group, SLAB * group), BF16),
            pltpu.VMEM((4, n, SLAB, lanes), BF16),
            pltpu.VMEM((4, n, SLAB, lanes), BF16),
            pltpu.VMEM((n, minor, 128), F32),
            pltpu.VMEM((n, minor, 128), F32),
            pltpu.SemaphoreType.DMA((4,)),
            pltpu.SemaphoreType.DMA((5,)),
            pltpu.SemaphoreType.DMA((5,)),
        ],
        compiler_params=pltpu.CompilerParams(
            collective_id=0, has_side_effects=True, vmem_limit_bytes=56 * 1024 * 1024
        ),
        name="exchange",
    )(
        tokens.reshape(images * patches, dim), phi_t, w_in[0], w_out[0],
        cotangent.reshape(images * patches, dim),
    )

    steps = 2 * images
    half = patches // 2
    turned = pl.BlockSpec((1, n, half), lambda j: (j // 2, 0, j % 2))
    image = pl.BlockSpec((n, dim), lambda j: (j // 2, 0))

    def fixed(*s):
        return pl.BlockSpec(s, lambda j: (0,) * len(s))

    mixed, grad_tokens, grad_a, grad_b = pl.pallas_call(
        outputs_kernel,
        grid=(steps,),
        out_shape=(
            shape(images, patches, dim), shape(images, patches, dim),
            shape(1, dim, hid), shape(1, hid, dim),
        ),
        in_specs=[
            pl.BlockSpec((count, dim // steps), lambda j: (0, j)),
            fixed(count, hid),
            pl.BlockSpec((count, hid // steps), lambda j: (0, j)),
            fixed(count, dim),
            turned, image, turned, turned, image,
            fixed(n, dim),
        ],
        out_specs=(
            pl.BlockSpec((1, half, dim), lambda j: (j // 2, j % 2, 0)),
            pl.BlockSpec((1, half, dim), lambda j: (j // 2, j % 2, 0)),
            pl.BlockSpec((1, dim // steps, hid), lambda j: (0, j, 0)),
            pl.BlockSpec((1, hid // steps, dim), lambda j: (0, j, 0)),
        ),
        compiler_params=pltpu.CompilerParams(vmem_limit_bytes=48 * 1024 * 1024),
        name="outputs",
    )(x, d_pre, hidden, grads, comb_b, so, disp_b, dl_b, dsi, phi_t)
    return (mixed, grad_tokens, gphi.reshape(dim, 1), grad_a, grad_b)


def solution(mesh):
    cols = mesh.shape["col"]
    n = mesh.shape["row"] * cols
    split = P(("row", "col"), None, None)
    return jax.shard_map(
        functools.partial(on_device, n, cols),
        mesh=mesh,
        in_specs=(split, P(), split, split, split),
        out_specs=(split, split, P(None, ("row", "col")), split, split),
        check_vma=False,
    )
```

time: 220 us -> 64.8 us (0.29)
  waiting for transfers between devices: 136 us -> 0 us
  Pallas kernels: 0 us -> 53.9 us
  matrix products: 38.9 us -> 0 us
  starting transfers between devices: 19.9 us -> 0 us
  between operations: 14.2 us -> 0.67 us
  other arithmetic: 2.51 us -> 0 us
    unnamed x2 -> x0, waiting for transfers between devices: 118 us -> none
    pallas_call x0 -> x2, Pallas kernels: none -> 53.9 us  [the longest x1 46.5 us: on_device(): pl.pallas_call(functools.partial(exchange_kernel, n, cols, images), out_s...]
    dot_general x15 -> x0, matrix products: 38.9 us -> none  [the longest x1 4.91 us: on_device(): jnp.einsum('rd,hd->rh', grad_rows, weight_b, preferred_element_type=f32)]
    all_to_all x4 -> x0, starting transfers between devices: 19.7 us -> none  [the longest x1 7.3 us: send_slots(): lax.all_to_all(slots, ('row', 'col'), split_axis=1, concat_axis=1, tiled=...]
    all_to_all x4 -> x0, waiting for transfers between devices: 18.7 us -> none  [the longest x1 6.71 us: send_slots(): lax.all_to_all(slots, ('row', 'col'), split_axis=1, concat_axis=1, tiled=...]
    unnamed x17 -> x21, local copies, waits for them, and re-layouts: 3.28 us -> 9.67 us
    sub x3 -> x0, other arithmetic: 2.51 us -> none  [the longest x1 1.04 us: on_device(): d_combine - jnp.sum(combine * d_combine, axis=2, keepdims=True)]
  transfers between devices with their start and end apart: 5 -> 0, of which waited for: 4 -> 0; matrix products, arithmetic and copies ran while one was open for 12% -> 0% of each run, Pallas kernels for 0% -> 0%
where the time goes in v2:
time: 64.8 us; the launch traced here: 64.3 us
  Pallas kernels  53.9 us (83%)
  local copies, waits for them, and re-layouts  9.67 us (15%)
  between operations  0.67 us (1%)
    pallas_call x1, Pallas kernels, on_device(): pl.pallas_call(functools.partial(exchange_kernel, n, cols, images), out_s...  46.5 us
    unnamed x21, local copies, waits for them, and re-layouts  9.67 us
    pallas_call x1, Pallas kernels, on_device(): pl.pallas_call(outputs_kernel, grid=(steps,), out_shape=(shape(images, pa...  7.49 us

profile of v2, /device:TPU:0, one launch (start us, length us, event | category | flops | bytes accessed | tf_op | source)
XLA Modules:
  0.0 64.3 jit_solution(18382333525442064247)
XLA Ops:
  0.6 0.0 copy-start.2
  0.6 46.5 %exchange.1 = (bf16[128,1024]{1,0:T(8,128)(2,1)}, bf16[128,2048]{1,0:T(8,128)(2,1)}, bf16[128,2048]{1,0:T(8,128)(2,1)}, bf16[128,1024]{1,0:T(8,128)(2,1)}, bf16[...) custom-call(bf16[1024,1024]{1,0:T(8,128)(2,1)} %bitcast.10, ...), custom_call_target="tpu_custom_call" | custom-call | tf_op jit(solution)/shard_map/exchange/pallas_call | solution.py:264
  47.1 0.0 copy-done.2
  47.1 0.0 copy-start
  47.1 1.0 %copy-done = bf16[128,2048]{1,0:T(8,128)(2,1)S(1)} copy-done((bf16[128,2048]{1,0:T(8,128)(2,1)S(1)}, bf16[128,2048]{1,0:T(8,128)(2,1)}, u32[]{:S(2)}) %copy-start) | copy-done | bytes 524312
  48.2 0.0 copy-start.1
  48.2 1.0 %copy-done.1 = bf16[128,2048]{1,0:T(8,128)(2,1)S(1)} copy-done((bf16[128,2048]{1,0:T(8,128)(2,1)S(1)}, bf16[128,2048]{1,0:T(8,128)(2,1)}, u32[]{:S(2)}) %copy-start.1) | copy-done | bytes 524312
  49.2 0.0 copy-start.3
  49.2 0.9 %copy-done.3 = bf16[128,1024]{1,0:T(8,128)(2,1)S(1)} copy-done((bf16[128,1024]{1,0:T(8,128)(2,1)S(1)}, bf16[128,1024]{1,0:T(8,128)(2,1)}, u32[]{:S(2)}) %copy-start.3) | copy-done | bytes 262168
  50.2 0.0 copy-start.4
  50.2 0.9 %copy-done.4 = bf16[128,1024]{1,0:T(8,128)(2,1)S(1)} copy-done((bf16[128,1024]{1,0:T(8,128)(2,1)S(1)}, bf16[128,1024]{1,0:T(8,128)(2,1)}, u32[]{:S(2)}) %copy-start.4) | copy-done | bytes 262168
  51.1 0.0 copy-start.5
  51.1 0.9 %copy-done.5 = bf16[128,1024]{1,0:T(8,128)(2,1)S(1)} copy-done((bf16[128,1024]{1,0:T(8,128)(2,1)S(1)}, bf16[128,1024]{1,0:T(8,128)(2,1)}, u32[]{:S(2)}) %copy-start.5) | copy-done | bytes 262168
  52.1 0.0 copy-start.6
  52.1 0.9 %copy-done.6 = bf16[128,1024]{1,0:T(8,128)(2,1)S(1)} copy-done((bf16[128,1024]{1,0:T(8,128)(2,1)S(1)}, bf16[128,1024]{1,0:T(8,128)(2,1)}, u32[]{:S(2)}) %copy-start.6) | copy-done | bytes 262168
  53.0 0.0 copy-start.7
  53.0 0.8 %copy-done.7 = bf16[4,32,256]{2,1,0:T(8,128)(2,1)S(1)} copy-done((bf16[4,32,256]{2,1,0:T(8,128)(2,1)S(1)}, bf16[4,32,256]{2,1,0:T(8,128)(2,1)}, u32[]{:S(2)}) %copy-start.7) | copy-done | bytes 65560
  53.8 0.0 copy-start.8
  53.9 0.8 %copy-done.8 = bf16[4,32,256]{2,1,0:T(8,128)(2,1)S(1)} copy-done((bf16[4,32,256]{2,1,0:T(8,128)(2,1)S(1)}, bf16[4,32,256]{2,1,0:T(8,128)(2,1)}, u32[]{:S(2)}) %copy-start.8) | copy-done | bytes 65560
  54.7 0.0 copy-start.9
  54.7 0.8 %copy-done.9 = bf16[4,32,256]{2,1,0:T(8,128)(2,1)S(1)} copy-done((bf16[4,32,256]{2,1,0:T(8,128)(2,1)S(1)}, bf16[4,32,256]{2,1,0:T(8,128)(2,1)}, u32[]{:S(2)}) %copy-start.9) | copy-done | bytes 65560
  55.5 7.5 %outputs.1 = (bf16[4,256,1024]{2,1,0:T(8,128)(2,1)}, bf16[4,256,1024]{2,1,0:T(8,128)(2,1)}, bf16[1,1024,2048]{2,1,0:T(8,128)(2,1)}, bf16[1,2048,1024]{2,1,0:T(8,128)(2,1)}) custom-call(bf16[128,1024]{1,0:T(8,128)(2,1)S(1)} %copy-done.3, bf16[128,2048]{1,0:T(8,128)(2,1)S(1)} %copy-done.1, bf16[128,2048]{1,0:T(8,128)(2,1)S(1)} %copy-done, ...), custom_call_target="tpu_custom_call" | custom-call | tf_op jit(solution)/shard_map/outputs/pallas_call | solution.py:310
  63.0 1.3 %copy.11 = f32[1024,1]{0,1:T(1,128)} copy(f32[1024,1]{0,1:T(1,128)} %bitcast.12) | data formatting | bytes 8192
Async XLA Ops:
  0.6 46.5 %copy-start.2 = (bf16[1024,32]{0,1:T(8,128)(2,1)S(1)}, bf16[1024,32]{0,1:T(8,128)(2,1)}, u32[]{:S(2)}) copy-start(bf16[1024,32]{0,1:T(8,128)(2,1)} %param.6) | copy-start | bytes 196612
  47.1 1.0 %copy-start = (bf16[128,2048]{1,0:T(8,128)(2,1)S(1)}, bf16[128,2048]{1,0:T(8,128)(2,1)}, u32[]{:S(2)}) copy-start(bf16[128,2048]{1,0:T(8,128)(2,1)} %get-tuple-element.21.hid_ref) | copy-start | bytes 1572868
  48.2 1.0 %copy-start.1 = (bf16[128,2048]{1,0:T(8,128)(2,1)S(1)}, bf16[128,2048]{1,0:T(8,128)(2,1)}, u32[]{:S(2)}) copy-start(bf16[128,2048]{1,0:T(8,128)(2,1)} %get-tuple-element.20.dpre_ref) | copy-start | bytes 1572868
  49.2 0.9 %copy-start.3 = (bf16[128,1024]{1,0:T(8,128)(2,1)S(1)}, bf16[128,1024]{1,0:T(8,128)(2,1)}, u32[]{:S(2)}) copy-start(bf16[128,1024]{1,0:T(8,128)(2,1)} %get-tuple-element.19.x_ref) | copy-start | bytes 786436
  50.2 0.9 %copy-start.4 = (bf16[128,1024]{1,0:T(8,128)(2,1)S(1)}, bf16[128,1024]{1,0:T(8,128)(2,1)}, u32[]{:S(2)}) copy-start(bf16[128,1024]{1,0:T(8,128)(2,1)} %get-tuple-element.22.g_ref) | copy-start | bytes 786436
  51.1 0.9 %copy-start.5 = (bf16[128,1024]{1,0:T(8,128)(2,1)S(1)}, bf16[128,1024]{1,0:T(8,128)(2,1)}, u32[]{:S(2)}) copy-start(bf16[128,1024]{1,0:T(8,128)(2,1)} %get-tuple-element.24.so_ref) | copy-start | bytes 786436
  52.1 0.9 %copy-start.6 = (bf16[128,1024]{1,0:T(8,128)(2,1)S(1)}, bf16[128,1024]{1,0:T(8,128)(2,1)}, u32[]{:S(2)}) copy-start(bf16[128,1024]{1,0:T(8,128)(2,1)} %get-tuple-element.27.dsi_ref) | copy-start | bytes 786436
  53.0 0.8 %copy-start.7 = (bf16[4,32,256]{2,1,0:T(8,128)(2,1)S(1)}, bf16[4,32,256]{2,1,0:T(8,128)(2,1)}, u32[]{:S(2)}) copy-start(bf16[4,32,256]{2,1,0:T(8,128)(2,1)} %get-tuple-element.25.disp_b) | copy-start | bytes 196612
  53.8 0.8 %copy-start.8 = (bf16[4,32,256]{2,1,0:T(8,128)(2,1)S(1)}, bf16[4,32,256]{2,1,0:T(8,128)(2,1)}, u32[]{:S(2)}) copy-start(bf16[4,32,256]{2,1,0:T(8,128)(2,1)} %get-tuple-element.23.comb_b) | copy-start | bytes 196612
  54.7 0.8 %copy-start.9 = (bf16[4,32,256]{2,1,0:T(8,128)(2,1)S(1)}, bf16[4,32,256]{2,1,0:T(8,128)(2,1)}, u32[]{:S(2)}) copy-start(bf16[4,32,256]{2,1,0:T(8,128)(2,1)} %get-tuple-element.26.dl_b) | copy-start | bytes 196612

commit v3 on v2

--- a/solution.py
+++ b/solution.py
@@ -73,8 +73,8 @@
             ((tok_hbm, tok), (cot_hbm, cot), (w_in_hbm, w_in), (w_out_hbm, w_out))
         )
     ]
-    for load in loads:
-        load.start()
+    loads[0].start()
+    loads[1].start()
 
     barrier = pltpu.get_barrier_semaphore()
 
@@ -128,9 +128,10 @@
                     ]
 
     perm[...] = permutation(SLAB, group)
-    perm_back[...] = permutation_back(SLAB, group)
 
     loads[0].wait()
+    loads[2].start()
+    loads[3].start()
     for i in range(images):
         mine = tok[i * patches : (i + 1) * patches]
         logits = dot(phi_t[...], mine, NT)
@@ -153,6 +154,7 @@
         rows[i * n : (i + 1) * n] = dot(comb_b[i], mine, NN).astype(BF16)
     pack(rows, sends.at[1])
     start(1, sends.at[1], recvs.at[1])
+    perm_back[...] = permutation_back(SLAB, group)
 
     loads[2].wait()
     loads[3].wait()
@@ -236,15 +238,40 @@
 
 
 def outputs_kernel(
-    x_ref, dpre_ref, hid_ref, g_ref, comb_b, so_ref, disp_b, dl_b, dsi_ref, phi_t,
-    mixed_ref, gtok_ref, gin_ref, gout_ref,
+    images,
+    x_ref, dpre_ref, hid_ref, g_ref, comb_b, so_ref, disp_b, dl_b, dsi_ref, phi_t, gphi_ref,
+    mixed_hbm, gtok_hbm, gin_hbm, gout_hbm, column_ref,
+    mixed, gtok, gin, gout, sem,
 ):
-    gin_ref[0] = dot(x_ref[...], dpre_ref[...], TN).astype(BF16)
-    gout_ref[0] = dot(hid_ref[...], g_ref[...], TN).astype(BF16)
-    mixed_ref[0] = dot(comb_b[0], so_ref[...], TN).astype(BF16)
-    left = jnp.concatenate([disp_b[0], dl_b[0]], axis=0)
-    right = jnp.concatenate([dsi_ref[...], phi_t[...]], axis=0)
-    gtok_ref[0] = dot(left, right, TN).astype(BF16)
+    n = phi_t.shape[0]
+    copies = []
+
+    def put(k, j, src, dst, size):
+        at = pl.ds(j * size, size)
+        copy = pltpu.make_async_copy(src.at[at], dst.at[at], sem.at[k, j])
+        copy.start()
+        copies.append(copy)
+
+    wide = gin.shape[0] // images
+    tall = gout.shape[0] // images
+    for j in range(images):
+        at = slice(j * wide, (j + 1) * wide)
+        gin[at] = dot(x_ref[:, at], dpre_ref[...], TN).astype(BF16)
+        put(0, j, gin, gin_hbm.at[0], wide)
+        at = slice(j * tall, (j + 1) * tall)
+        gout[at] = dot(hid_ref[:, at], g_ref[...], TN).astype(BF16)
+        put(1, j, gout, gout_hbm.at[0], tall)
+        at = slice(j * n, (j + 1) * n)
+        mixed[j] = dot(comb_b[j], so_ref[at], TN).astype(BF16)
+        put(2, j, mixed, mixed_hbm, 1)
+        left = jnp.concatenate([disp_b[j], dl_b[j]], axis=0)
+        right = jnp.concatenate([dsi_ref[at], phi_t[...]], axis=0)
+        gtok[j] = dot(left, right, TN).astype(BF16)
+        put(3, j, gtok, gtok_hbm, 1)
+    for j in range(gphi_ref.shape[0]):
+        column_ref[:, j * 128 : (j + 1) * 128] = gphi_ref[j : j + 1, :]
+    for copy in copies:
+        copy.wait()
 
 
 def on_device(n, cols, tokens, phi, w_in, w_out, cotangent):
@@ -299,39 +326,25 @@
         cotangent.reshape(images * patches, dim),
     )
 
-    steps = 2 * images
-    half = patches // 2
-    turned = pl.BlockSpec((1, n, half), lambda j: (j // 2, 0, j % 2))
-    image = pl.BlockSpec((n, dim), lambda j: (j // 2, 0))
-
-    def fixed(*s):
-        return pl.BlockSpec(s, lambda j: (0,) * len(s))
-
-    mixed, grad_tokens, grad_a, grad_b = pl.pallas_call(
-        outputs_kernel,
-        grid=(steps,),
+    mixed, grad_tokens, grad_a, grad_b, grad_phi = pl.pallas_call(
+        functools.partial(outputs_kernel, images),
         out_shape=(
             shape(images, patches, dim), shape(images, patches, dim),
-            shape(1, dim, hid), shape(1, hid, dim),
+            shape(1, dim, hid), shape(1, hid, dim), shape(1, dim, t=F32),
         ),
-        in_specs=[
-            pl.BlockSpec((count, dim // steps), lambda j: (0, j)),
-            fixed(count, hid),
-            pl.BlockSpec((count, hid // steps), lambda j: (0, j)),
-            fixed(count, dim),
-            turned, image, turned, turned, image,
-            fixed(n, dim),
+        in_specs=[vmem] * 11,
+        out_specs=(any_,) * 4 + (vmem,),
+        scratch_shapes=[
+            pltpu.VMEM((images, patches, dim), BF16),
+            pltpu.VMEM((images, patches, dim), BF16),
+            pltpu.VMEM((dim, hid), BF16),
+            pltpu.VMEM((hid, dim), BF16),
+            pltpu.SemaphoreType.DMA((4, images)),
         ],
-        out_specs=(
-            pl.BlockSpec((1, half, dim), lambda j: (j // 2, j % 2, 0)),
-            pl.BlockSpec((1, half, dim), lambda j: (j // 2, j % 2, 0)),
-            pl.BlockSpec((1, dim // steps, hid), lambda j: (0, j, 0)),
-            pl.BlockSpec((1, hid // steps, dim), lambda j: (0, j, 0)),
-        ),
-        compiler_params=pltpu.CompilerParams(vmem_limit_bytes=48 * 1024 * 1024),
+        compiler_params=pltpu.CompilerParams(vmem_limit_bytes=63 * 1024 * 1024 + 768 * 1024),
         name="outputs",
-    )(x, d_pre, hidden, grads, comb_b, so, disp_b, dl_b, dsi, phi_t)
-    return (mixed, grad_tokens, gphi.reshape(dim, 1), grad_a, grad_b)
+    )(x, d_pre, hidden, grads, comb_b, so, disp_b, dl_b, dsi, phi_t, gphi)
+    return (mixed, grad_tokens, grad_phi.reshape(dim, 1), grad_a, grad_b)
 
 
 def solution(mesh):

time: 64.8 us -> 54.6 us (0.84)
  local copies, waits for them, and re-layouts: 9.67 us -> 0 us
    unnamed x21 -> x0, local copies, waits for them, and re-layouts: 9.67 us -> none
where the time goes in v3:
time: 54.6 us; the launch traced here: 54.4 us
  Pallas kernels  53.7 us (98%)
  between operations  0.64 us (1%)
    pallas_call x1, Pallas kernels, on_device(): pl.pallas_call(functools.partial(exchange_kernel, n, cols, images), out_s...  46.4 us
    pallas_call x1, Pallas kernels, on_device(): pl.pallas_call(functools.partial(outputs_kernel, images), out_shape=(shap...  7.32 us

profile of v3, /device:TPU:0, one launch (start us, length us, event | category | flops | bytes accessed | tf_op | source)
XLA Modules:
  0.0 54.4 jit_solution(3351321253766420829)
XLA Ops:
  0.6 46.4 %exchange.1 = (bf16[128,1024]{1,0:T(8,128)(2,1)}, bf16[128,2048]{1,0:T(8,128)(2,1)}, bf16[128,2048]{1,0:T(8,128)(2,1)}, bf16[128,1024]{1,0:T(8,128)(2,1)}, bf16[...) custom-call(bf16[1024,1024]{1,0:T(8,128)(2,1)} %bitcast.8, ...), custom_call_target="tpu_custom_call" | custom-call | tf_op jit(solution)/shard_map/exchange/pallas_call | solution.py:291
  47.1 7.3 %outputs.1 = (bf16[4,256,1024]{2,1,0:T(8,128)(2,1)}, bf16[4,256,1024]{2,1,0:T(8,128)(2,1)}, bf16[1,1024,2048]{2,1,0:T(8,128)(2,1)}, bf16[1,2048,1024]{2,1,0:T(8,128)(2,1)}, f32[1,1024]{1,0:T(1,128)}) custom-call(bf16[128,1024]{1,0:T(8,128)(2,1)} %get-tuple-element.20.x_ref, bf16[128,2048]{1,0:T(8,128)(2,1)} %get-tuple-element.21.dpre_ref, ...), custom_call_target="tpu_custom_call" | custom-call | tf_op jit(solution)/shard_map/outputs/pallas_call | solution.py:329

commit v4 on v3

--- a/solution.py
+++ b/solution.py
@@ -83,11 +83,13 @@
         pl.semaphore_signal(barrier, inc=1, device_id=(d // cols, lax.rem(d, cols)), device_id_type=MESH)
         return carry
 
-    lax.fori_loop(1, n, greet, 0)
+    lax.fori_loop(1, n, greet, 0, unroll=n <= 32)
 
     def start(k, src, dst):
+        stride = 13 if math.gcd(13, n) == 1 else 1
+
         def one(j, carry):
-            d = lax.rem(me + j, n)
+            d = lax.rem(me + j * stride, n)
             pltpu.make_async_remote_copy(
                 src_ref=src.at[d], dst_ref=dst.at[me],
                 send_sem=send_sem.at[k], recv_sem=recv_sem.at[k],
@@ -95,7 +97,7 @@
             ).start()
             return carry
 
-        lax.fori_loop(1, n, one, 0)
+        lax.fori_loop(1, n, one, 0, unroll=n <= 32)
         dst[me] = src[me]
 
     def whole(k, src, dst):
@@ -167,9 +169,9 @@
     @pl.loop(0, hid // wide)
     def _(c):
         at = pl.ds(pl.multiple_of(c * wide, wide), wide)
-        value, grad = gelu_parts(dot(x_ref[...], w_in[:, at], NN))
-        hid_ref[:, at] = value.astype(BF16)
-        slope[:, at] = grad
+        pre_act = dot(x_ref[...], w_in[:, at], NN)
+        hid_ref[:, at] = gelu_parts(pre_act)[0].astype(BF16)
+        slope[:, at] = pre_act
 
     @pl.loop(0, dim // thin)
     def _(c):
@@ -178,6 +180,11 @@
 
     pack(rows, sends.at[2])
     start(2, sends.at[2], recvs.at[2])
+
+    @pl.loop(0, hid // wide)
+    def _(c):
+        at = pl.ds(pl.multiple_of(c * wide, wide), wide)
+        slope[:, at] = gelu_parts(slope[:, at])[1]
 
     whole(1, sends.at[1], recvs.at[1]).wait_recv()
     unpack(recvs.at[1], g_ref)

time: 54.6 us -> 53.4 us (0.978)
  Pallas kernels: 53.7 us -> 52.6 us
    pallas_call x1, Pallas kernels: 46.4 us -> 45.3 us  [on_device(): pl.pallas_call(functools.partial(exchange_kernel, n, cols, images), out_s...]
where the time goes in v4:
time: 53.4 us; the launch traced here: 53.2 us
  Pallas kernels  52.6 us (99%)
  between operations  0.64 us (1%)
    pallas_call x1, Pallas kernels, on_device(): pl.pallas_call(functools.partial(exchange_kernel, n, cols, images), out_s...  45.3 us
    pallas_call x1, Pallas kernels, on_device(): pl.pallas_call(functools.partial(outputs_kernel, images), out_shape=(shap...  7.31 us

profile of v4, /device:TPU:0, one launch (start us, length us, event | category | flops | bytes accessed | tf_op | source)
XLA Modules:
  0.0 53.2 jit_solution(16460430981468651162)
XLA Ops:
  0.6 45.3 %exchange.1 = (bf16[128,1024]{1,0:T(8,128)(2,1)}, bf16[128,2048]{1,0:T(8,128)(2,1)}, bf16[128,2048]{1,0:T(8,128)(2,1)}, bf16[128,1024]{1,0:T(8,128)(2,1)}, bf16[...) custom-call(bf16[1024,1024]{1,0:T(8,128)(2,1)} %bitcast.8, ...), custom_call_target="tpu_custom_call" | custom-call | tf_op jit(solution)/shard_map/exchange/pallas_call | solution.py:298
  45.9 7.3 %outputs.1 = (bf16[4,256,1024]{2,1,0:T(8,128)(2,1)}, bf16[4,256,1024]{2,1,0:T(8,128)(2,1)}, bf16[1,1024,2048]{2,1,0:T(8,128)(2,1)}, bf16[1,2048,1024]{2,1,0:T(8,128)(2,1)}, f32[1,1024]{1,0:T(1,128)}) custom-call(bf16[128,1024]{1,0:T(8,128)(2,1)} %get-tuple-element.20.x_ref, bf16[128,2048]{1,0:T(8,128)(2,1)} %get-tuple-element.21.dpre_ref, ...), custom_call_target="tpu_custom_call" | custom-call | tf_op jit(solution)/shard_map/outputs/pallas_call | solution.py:336
